TPU v7x, 128 devices: a whole 4x4x4 slice. The times are simulated.
128 devices in a mesh: wide: 16 (over x, z), narrow: 8 (over y, core).
Axes of the slice: x: 4, y: 4, z: 4, core: 2. Of those that a mesh axis runs over, the one named last changes fastest.
Arguments:
- tensor: bfloat16 [16, 128, 64, 16, 128], P('wide', None, 'narrow'), may hold values from -6 to 6
- tensor_mask: int32 [16, 16], P('wide'), may hold values 0 or 1
- occ_density: bfloat16 [16, 128, 16, 128], P('wide', None, 'narrow'), may hold values from -0.125 to 0.125
- occ_mask: int32 [16, 16], P('wide', 'narrow'), may hold values 0 or 1
- virt_density: bfloat16 [16, 128, 16, 128], P('wide', None, 'narrow'), may hold values from -0.125 to 0.125
- virt_mask: int32 [16, 16], P('wide', 'narrow'), may hold values 0 or 1
Outputs:
- contracted: bfloat16 [16, 128, 64, 16, 128], P(None, None, 'narrow', 'wide')
All inputs are finite; a program needn't handle non-finite values. No bound on the sum of `tensor_mask` or of `occ_mask` or of `virt_mask` on one device may be relied on, other than what follows from the above.
Results may differ from a plain program's by a relative error of at most 0.0049.
Values may be sent and summed in bfloat16 or wider, within the bound.
A program may use at most 128 MiB of HBM per device.

v0:
```python
import jax
import jax.numpy as jnp
from jax import lax
from jax.sharding import PartitionSpec as P


def shards(tensor, tensor_mask, occ_density, occ_mask, virt_density, virt_mask):
    block_size = tensor.shape[1]
    rank_local = tensor.shape[2]
    block_count = tensor.shape[3]
    wide_count = lax.axis_size("wide")
    narrow_count = lax.axis_size("narrow")
    masked_tensor = tensor * tensor_mask.astype(tensor.dtype)[:, None, None, :, None]
    tensor_flat = masked_tensor.reshape(block_size * rank_local, block_count * block_size)
    occ_local = occ_density * occ_mask.astype(occ_density.dtype)[:, None, :, None]
    virt_local = virt_density * virt_mask.astype(virt_density.dtype)[:, None, :, None]
    occ_tiles, virt_tiles = (
        lax.all_gather(occ_local[None], ("wide", "narrow"), axis=0, tiled=True),
        lax.all_gather(virt_local[None], ("wide", "narrow"), axis=0, tiled=True),
    )
    column_blocks = block_count // narrow_count

    def assemble(tiles):
        grid_tiles = tiles.reshape(wide_count, narrow_count, block_size, column_blocks, block_size)
        ordered = jnp.transpose(grid_tiles, (0, 2, 1, 3, 4))
        return ordered.reshape(block_count * block_size, block_count * block_size)

    occ_full = assemble(occ_tiles)
    virt_full = assemble(virt_tiles)
    first_sum = jnp.dot(tensor_flat, occ_full, preferred_element_type=jnp.float32)
    half_moved = first_sum.astype(jnp.bfloat16).reshape(
        1, block_size, rank_local, block_count, block_size
    )
    remapped = lax.all_to_all(half_moved, "wide", split_axis=3, concat_axis=0, tiled=True)
    remap_flat = remapped.reshape(block_count * block_size, rank_local * block_size)
    second_sum = jnp.dot(virt_full, remap_flat, preferred_element_type=jnp.float32)
    return second_sum.astype(jnp.bfloat16).reshape(
        block_count, block_size, rank_local, 1, block_size
    )


def solution(mesh):
    placed = (
        P("wide", None, "narrow", None, None),
        P("wide", None),
        P("wide", None, "narrow", None),
        P("wide", "narrow"),
        P("wide", None, "narrow", None),
        P("wide", "narrow"),
    )
    return jax.shard_map(
        shards,
        mesh=mesh,
        in_specs=placed,
        out_specs=P(None, None, "narrow", "wide", None),
        check_vma=False,
    )
```

profile of v0, /device:TPU:1, one launch (start us, length us, event | category | flops | bytes accessed | tf_op | source)
XLA Modules:
  0.0 224.7 jit_solution(11455150489726810045)
XLA Ops:
  6.5 0.0 all-gather.7.cloned.1.call-start
  6.5 0.7 convert_bitcast_fusion.2
  7.2 1.5 copy_multiply_fusion
  8.7 0.0 all-gather.7.cloned.1.call-update
  8.8 0.0 all-gather.5.cloned.1.call-start
  8.8 0.7 convert_bitcast_fusion.4
  9.5 1.5 copy_multiply_fusion.1
  11.0 0.0 all-gather.5.cloned.1.call-update
  11.0 0.7 convert_bitcast_fusion.3
  11.7 4.5 %multiply_bitcast_fusion = bf16[128,8,16,128]{3,2,1,0:T(8,128)(2,1)} fusion(bf16[1,128,8,16,128]{4,3,2,1,0:T(8,128)(2,1)} %param.6, bf16[16]{0:T(256)(128)(2,1)S(1)} %convert_bitcast_fusion.3), kind=kLoop, calls=%fused_computation.12 | loop fusion | flops 2097152 | bytes 8388640
  16.2 67.9 %all-gather.7.cloned.1.call-done = bf16[128,128,2,128]{3,1,2,0:T(8,128)(2,1)} async-done(((bf16[1,128,2,128]{3,1,2,0:T(8,128)(2,1)}), bf16[128,128,2,128]{3,1,2,0:T(8,128)(2,1)}) %all-gather.7.cloned.1.call-update) | async-done | bytes 8388624 | tf_op jit(solution)/shard_map/all_gather | solution.py:18
  84.1 12.7 %copy.15 = bf16[16,8,128,2,128]{2,0,4,3,1:T(8,128)(2,1)} copy(bf16[16,8,128,2,128]{4,2,3,1,0:T(8,128)(2,1)} %bitcast.57) | data formatting | bytes 16777216 | tf_op jit(solution)/shard_map/reshape | solution.py:24
  96.8 12.6 %convert_bitcast_fusion.1 = bf16[1,128,8,16,128]{4,2,3,1,0:T(8,128)(2,1)S(1)} fusion(bf16[256,8,16,128]{3,2,1,0:T(8,128)(2,1)} %bitcast.59, bf16[128,8,16,128]{3,2,1,0:T(8,128)(2,1)} %multiply_bitcast_fusion), kind=kOutput, calls=%fused_computation.11 | convolution fusion | flops 8592031744 | bytes 16777216 | tf_op jit(solution)/shard_map/dot_general | solution.py:30
  109.5 3.1 %copy.16 = bf16[1,128,8,16,128]{4,2,1,0,3:T(8,128)(2,1)} copy(bf16[1,128,8,16,128]{4,2,3,1,0:T(8,128)(2,1)S(1)} %convert_bitcast_fusion.1) | data formatting | bytes 8388608 | tf_op jit(solution)/shard_map/reshape | solution.py:31
  112.6 4.8 %all-to-all-start = ((bf16[1,128,8,16,128]{4,2,1,0,3:T(8,128)(2,1)}), bf16[1,128,8,16,128]{4,2,1,0,3:T(8,128)(2,1)}, u32[]{:S(2)}, u32[]{:S(2)}) async-start(bf16[1,128,8,16,128]{4,2,1,0,3:T(8,128)(2,1)} %copy.16), calls=%async_computation | async-start | bytes 8388608 | tf_op jit(solution)/shard_map/all_to_all | solution.py:34
  117.4 72.2 %all-gather.5.cloned.1.call-done = bf16[128,128,2,128]{3,1,2,0:T(8,128)(2,1)} async-done(((bf16[1,128,2,128]{3,1,2,0:T(8,128)(2,1)}), bf16[128,128,2,128]{3,1,2,0:T(8,128)(2,1)}) %all-gather.5.cloned.1.call-update) | async-done | bytes 8388624 | tf_op jit(solution)/shard_map/all_gather | solution.py:19
  189.6 12.4 %copy.13 = bf16[16,8,128,2,128]{2,0,4,3,1:T(8,128)(2,1)} copy(bf16[16,8,128,2,128]{4,2,3,1,0:T(8,128)(2,1)} %bitcast.56) | data formatting | bytes 16777216 | tf_op jit(solution)/shard_map/reshape | solution.py:24
  202.1 0.0 all-to-all-done
  202.1 12.7 %convert_bitcast_fusion = bf16[256,8,8,128]{3,1,2,0:T(8,128)(2,1)S(1)} fusion(bf16[256,8,8,128]{3,2,1,0:T(8,128)(2,1)} %bitcast.27, bf16[256,8,16,128]{3,2,1,0:T(8,128)(2,1)} %bitcast.58), kind=kOutput, calls=%fused_computation.10 | convolution fusion | flops 8592031744 | bytes 16777216 | tf_op jit(solution)/shard_map/dot_general | solution.py:36
  214.8 3.1 %copy.22 = bf16[256,8,8,128]{3,2,1,0:T(8,128)(2,1)} copy(bf16[256,8,8,128]{3,1,2,0:T(8,128)(2,1)S(1)} %convert_bitcast_fusion) | data formatting | bytes 8388608
Async XLA Ops:
  6.5 77.6 %all-gather.7.cloned.1.call-start = ((), (), s32[]{:S(2)}) async-start(), calls=%async_computation.2 | async-start | bytes 8454144 | tf_op jit(solution)/shard_map/all_gather | solution.py:18
  8.8 180.8 %all-gather.5.cloned.1.call-start = ((), (), s32[]{:S(2)}) async-start(), calls=%async_computation.1 | async-start | bytes 8454144 | tf_op jit(solution)/shard_map/all_gather | solution.py:19
  112.6 89.5 %all-to-all-start = ((bf16[1,128,8,16,128]{4,2,1,0,3:T(8,128)(2,1)}), bf16[1,128,8,16,128]{4,2,1,0,3:T(8,128)(2,1)}, u32[]{:S(2)}, u32[]{:S(2)}) async-start(bf16[1,128,8,16,128]{4,2,1,0,3:T(8,128)(2,1)} %copy.16), calls=%async_computation | async-start | bytes 8388608 | tf_op jit(solution)/shard_map/all_to_all | solution.py:34
Sparse Core Ops, SparseCore 0:
  10.3 73.7 all-gather.6
  87.1 102.4 all-gather.4
where the time goes:
time: 229 us; the launch traced here: 225 us
  waiting for transfers between devices  140 us (61%)
  local copies, waits for them, and re-layouts  31.4 us (14%)
  matrix products  25.3 us (11%)
  between operations  13.4 us (6%)
  other arithmetic  9.58 us (4%)
  starting transfers between devices  4.81 us (2%)
    all_gather x1, waiting for transfers between devices, shards(): lax.all_gather(virt_local[None], ('wide', 'narrow'), axis=0, tiled=True)  72.2 us
    all_gather x1, waiting for transfers between devices, shards(): lax.all_gather(occ_local[None], ('wide', 'narrow'), axis=0, tiled=True)  67.9 us
    reshape x2, local copies, waits for them, and re-layouts, assemble(): tiles.reshape(wide_count, narrow_count, block_size, column_blocks, block_...  25.2 us
    dot_general x1, matrix products, shards(): jnp.dot(virt_full, remap_flat, preferred_element_type=jnp.float32)  12.7 us
    dot_general x1, matrix products, shards(): jnp.dot(tensor_flat, occ_full, preferred_element_type=jnp.float32)  12.6 us
    all_to_all x1, starting transfers between devices, shards(): lax.all_to_all(half_moved, 'wide', split_axis=3, concat_axis=0, tiled=True)  4.76 us
  transfers between devices with their start and end apart: 3, of which 2 were waited for; matrix products, arithmetic and copies ran while one was open for 21% of the time, Pallas kernels for 0%

commit v1 on v0

v1 whole, which is shorter than its diff:
```python
import functools

import jax
import jax.numpy as jnp
from jax import lax
from jax.experimental import pallas as pl
from jax.experimental.pallas import tpu as pltpu
from jax.sharding import PartitionSpec as P

MESH = pl.DeviceIdType.MESH
BF16 = jnp.bfloat16
F32 = jnp.float32
S = 128
NB = 16
PL = 8
ROUNDS = 4
ROWS = 2 * PL * S


def ring(v):
    return lax.rem(v + 4, 4)


def kernel(
    t_hbm, tmask, occ_ref, omask, virt_ref, vmask, out_hbm,
    traw, tm, occ, acc, send, recv, virt, outv, perm,
    t_sem, x_ssem, x_rsem, o1_ssem, o1_rsem, o_ssem, o_rsem,
    v1_ssem, v1_rsem, v2_ssem, v2_rsem, v3_ssem, v3_rsem,
    a_ssem, a_rsem, out_sem,
):
    w = lax.axis_index("wide")
    n = lax.axis_index("narrow")
    x, z = w // 4, lax.rem(w, 4)
    y, k = n // 2, lax.rem(n, 2)

    def remote(src, dst, ssem, rsem, wide, narrow):
        return pltpu.make_async_remote_copy(
            src_ref=src, dst_ref=dst, send_sem=ssem, recv_sem=rsem,
            device_id=(wide, narrow), device_id_type=MESH,
        )

    def wait_rows(sem, rows):
        view = virt.at[pl.ds(0, rows), :]
        pltpu.make_async_copy(view, view, sem).wait()

    barrier = pltpu.get_barrier_semaphore()
    for d in range(1, 4):
        pl.semaphore_signal(barrier, inc=1, device_id=(w, ring(y + d) * 2 + k), device_id_type=MESH)
    for d in range(1, 16):
        for e in range(2):
            pl.semaphore_signal(
                barrier, inc=1, device_id=(lax.rem(w + d, 16), y * 2 + e), device_id_type=MESH
            )
    pl.semaphore_signal(barrier, inc=1, device_id=(w, y * 2 + 1 - k), device_id_type=MESH)

    for p in range(PL):
        pltpu.make_async_copy(t_hbm.at[:, p], traw.at[p], t_sem.at[p]).start()

    ycol = pl.ds(pl.multiple_of(y * S, S), S)
    ncol = pl.ds(pl.multiple_of(n * 2 * S, 2 * S), 2 * S)
    wrow = pl.ds(pl.multiple_of(w * S, S), S)
    for j in range(2):
        block = occ_ref[:, j, :].astype(F32) * omask[0, j].astype(F32)
        occ[j, w, :, ycol] = block.astype(BF16)
    for j in range(2):
        block = virt_ref[:, j, :].astype(F32) * vmask[0, j].astype(F32)
        virt[wrow, pl.ds(pl.multiple_of(n * 2 * S + j * S, S), S)] = block.astype(BF16)

    row = lax.broadcasted_iota(jnp.int32, (256, 256), 0)
    col = lax.broadcasted_iota(jnp.int32, (256, 256), 1)
    scale = jnp.zeros((256, 256), F32)
    for b in range(NB):
        scale = scale + jnp.where((row >> 4) == b, 1.0, 0.0) * tmask[0, b].astype(F32)
    hit = jnp.logical_and((row >> 4) == (col & 15), (row & 15) == (col >> 4))
    perm[...] = jnp.where(hit, scale, 0.0).astype(BF16)

    pl.semaphore_wait(barrier, 34)

    for d in (1, 3, 2):
        for i in range(2):
            own = occ.at[i, w, :, ycol]
            remote(own, own, o1_ssem, o1_rsem, w, ring(y + d) * 2 + k).start()
    for d in range(1, 16):
        own = virt.at[wrow, ncol]
        remote(own, own, v1_ssem, v1_rsem, lax.rem(w + d, 16), n).start()

    def own_rows(r):
        return pl.ds(pl.multiple_of(r * 512 + k * 256, 256), 256)

    def relayout(r):
        for pi in range(2):
            p = 2 * r + pi
            pltpu.make_async_copy(t_hbm.at[:, p], traw.at[p], t_sem.at[p]).wait()

            def body(g, c, p=p, pi=pi):
                pair = jnp.concatenate(
                    [
                        traw[p, pl.ds(pl.multiple_of(g * 32 + h * 16, 16), 16)].reshape(256, S)
                        for h in range(2)
                    ],
                    axis=1,
                )
                got = jnp.dot(perm[...], pair, preferred_element_type=F32).astype(BF16)
                for h in range(2):
                    first = r * 512 + k * 256 + pi * S + g * 32 + h * 16
                    tm[:, pl.ds(pl.multiple_of(first, 16), 16), :] = got[:, h * S : (h + 1) * S].reshape(
                        NB, 16, S
                    )
                return c

            lax.fori_loop(0, 4, body, 0)
        mine = tm.at[:, own_rows(r), :]
        remote(mine, mine, x_ssem.at[r], x_rsem.at[r], w, y * 2 + 1 - k).start()

    relayout(0)

    place = ((x, z), (z, x))

    def at(i, p, q):
        return p * 4 + q if i == 0 else q * 4 + p

    def pass_block(i, b, p, q):
        remote(occ.at[i, b], occ.at[i, b], o_ssem, o_rsem.at[i, b], at(i, p, q), n).start()

    def wait_block(i, b):
        pltpu.make_async_copy(occ.at[i, b], occ.at[i, b], o_rsem.at[i, b]).wait()

    wait_rows(o1_rsem, 48)
    for d in (1, 3, 2):
        for i in range(2):
            p, q = place[i]
            pass_block(i, w, ring(p + d), q)
    for i in range(2):
        p, q = place[i]
        for d in (1, 3):
            pass_block(i, w, p, ring(q + d))

    relayout(1)
    for d in (1, 3, 2):
        for i in range(2):
            p, q = place[i]
            b = at(i, ring(p + d), q)
            wait_block(i, b)
            for f in (1, 3):
                pass_block(i, b, p, ring(q + f))
    relayout(2)
    relayout(3)

    halves = [pl.ds(0, ROWS // 2), pl.ds(ROWS // 2, ROWS // 2)]

    def columns(yy, kk):
        return pl.ds(pl.multiple_of((yy * 2 + kk) * 2 * S, 2 * S), 2 * S)

    def to_core(yy, h):
        part = virt.at[halves[h], columns(yy, k)]
        remote(part, part, v3_ssem, v3_rsem, w, y * 2 + 1 - k).start()

    def along(yy, h, d, s):
        part = virt.at[halves[h], columns(yy, k)]
        remote(part, part, v2_ssem.at[s], v2_rsem.at[lax.rem(yy, 4), h], w, ring(y + d) * 2 + k).start()

    def wait_along(yy, h):
        part = virt.at[halves[h], columns(yy, k)]
        pltpu.make_async_copy(part, part, v2_rsem.at[yy, h]).wait()

    wait_rows(v1_rsem, 15 * 16)
    along(y, 0, 3, 0)
    along(y, 1, 1, 1)
    along(y, 1, 3, 2)
    along(y, 0, 1, 3)
    to_core(y, 0)
    to_core(y, 1)

    def product(i, bs, rows):
        lhs = jnp.concatenate([tm[b, rows, :] for b in bs], axis=1)
        rhs = jnp.concatenate([occ[i, b] for b in bs], axis=0)
        return jnp.dot(lhs, rhs, preferred_element_type=F32)

    def group(i, d):
        p, q = place[i]
        return [at(i, ring(p + f), ring(q + d)) for f in range(4)]

    def accumulate(d, first, cores):
        def body(r, c):
            for e in cores:
                rows = pl.ds(pl.multiple_of(r * 512 + e * 256, 256), 256)
                for i in range(2):
                    got = product(i, group(i, d), rows)
                    acc[i, rows, :] = got if first else acc[i, rows, :] + got
            return c

        lax.fori_loop(0, ROUNDS, body, 0)

    accumulate(0, True, [k])
    for i in range(2):
        p, q = place[i]
        for f in (0, 1):
            b = at(i, ring(p + f), ring(q + 1))
            wait_block(i, b)
            pass_block(i, b, p, ring(q + 3))
        for f in (3, 2):
            b = at(i, ring(p + f), ring(q + 3))
            wait_block(i, b)
            pass_block(i, b, p, ring(q + 1))
    for r in range(ROUNDS):
        theirs = tm.at[:, pl.ds(pl.multiple_of(r * 512 + (1 - k) * 256, 256), 256), :]
        pltpu.make_async_copy(theirs, theirs, x_rsem.at[r]).wait()
    accumulate(0, True, [1 - k])
    for i in range(2):
        p, q = place[i]
        for f in (3, 2):
            wait_block(i, at(i, ring(p + f), ring(q + 1)))
    accumulate(1, False, [0, 1])
    for i in range(2):
        p, q = place[i]
        for f in (0, 1):
            wait_block(i, at(i, ring(p + f), ring(q + 3)))
    accumulate(3, False, [0, 1])
    for i in range(2):
        p, q = place[i]
        for f in range(4):
            wait_block(i, at(i, ring(p + f), ring(q + 2)))

    def finish(r, c):
        for i in range(2):
            for e in range(2):
                rows = pl.ds(pl.multiple_of(r * 512 + e * 256, 256), 256)
                got = (acc[i, rows, :] + product(i, group(i, 2), rows)).astype(BF16)
                for xx in range(4):
                    for pi in range(2):
                        send[r, i, xx, e, :, pi * S : (pi + 1) * S] = got[
                            pi * S : (pi + 1) * S, xx * S : (xx + 1) * S
                        ]
        for d in (1, 3, 2, 0):
            xx = ring(x + d)
            for j in range(2):
                i = lax.rem(j + z, 2)
                for e in range(2):
                    wide = xx * 4 + 2 * k + i
                    here = jnp.logical_and(wide == w, k == e)
                    src = send.at[r, i, xx, e]
                    dst = recv.at[r, wrow, :]

                    def away(src=src, dst=dst, wide=wide, e=e):
                        remote(src, dst, a_ssem.at[r], a_rsem.at[r], wide, y * 2 + e).start()

                    if d == 0:
                        pl.when(jnp.logical_not(here))(away)

                        @pl.when(here)
                        def _(src=src, dst=dst):
                            pltpu.make_async_copy(src, dst, a_rsem.at[r]).start()
                    else:
                        away()
        return c

    lax.fori_loop(0, ROUNDS, finish, 0)

    up, down, far = ring(y + 1), ring(y + 3), ring(y + 2)
    wait_along(up, 0)
    along(up, 0, 3, 4)
    to_core(up, 0)
    wait_along(down, 1)
    along(down, 1, 1, 5)
    to_core(down, 1)
    wait_along(up, 1)
    to_core(up, 1)
    wait_along(down, 0)
    to_core(down, 0)
    wait_along(far, 0)
    to_core(far, 0)
    wait_along(far, 1)
    to_core(far, 1)
    wait_rows(v3_rsem, ROWS // 2)

    def second(r, c):
        pltpu.make_async_copy(recv.at[r], recv.at[r], a_rsem.at[r]).wait()

        def chunk(m, cc):
            rows = pl.ds(pl.multiple_of(m * 256, 256), 256)
            got = jnp.dot(virt[rows, :], recv[r], preferred_element_type=F32).astype(BF16)
            for pi in range(2):
                outv[2 * r + pi, rows, :] = got[:, pi * S : (pi + 1) * S]
            part = outv.at[pl.ds(2 * r, 2), rows, :]
            pltpu.make_async_copy(part, out_hbm.at[pl.ds(2 * r, 2), rows, :], out_sem).start()
            return cc

        lax.fori_loop(0, 8, chunk, 0)
        return c

    lax.fori_loop(0, ROUNDS, second, 0)

    pltpu.make_async_copy(outv, out_hbm, out_sem).wait()
    wait_rows(o1_ssem, 48)
    wait_rows(o_ssem, 960)
    wait_rows(v1_ssem, 15 * 16)
    for s in range(6):
        part = virt.at[halves[0], pl.ds(0, 2 * S)]
        pltpu.make_async_copy(part, part, v2_ssem.at[s]).wait()
    wait_rows(v3_ssem, ROWS // 2)
    for r in range(ROUNDS):
        mine = tm.at[:, own_rows(r), :]
        pltpu.make_async_copy(mine, mine, x_ssem.at[r]).wait()
        local = z // 2 == k

        @pl.when(local)
        def _(r=r):
            wait_rows(a_ssem.at[r], 15 * 16)

        @pl.when(jnp.logical_not(local))
        def _(r=r):
            wait_rows(a_ssem.at[r], 16 * 16)


def shards(tensor, tensor_mask, occ_density, occ_mask, virt_density, virt_mask):
    dma = pltpu.SemaphoreType.DMA
    vmem, smem = pl.BlockSpec(memory_space=pltpu.VMEM), pl.BlockSpec(memory_space=pltpu.SMEM)
    out = pl.pallas_call(
        kernel,
        out_shape=jax.ShapeDtypeStruct((PL, NB * S, S), BF16),
        in_specs=[pl.BlockSpec(memory_space=pl.ANY), smem, vmem, smem, vmem, smem],
        out_specs=pl.BlockSpec(memory_space=pl.ANY),
        scratch_shapes=[
            pltpu.VMEM((PL, S, NB, S), BF16),
            pltpu.VMEM((NB, ROWS, S), BF16),
            pltpu.VMEM((2, NB, S, 4 * S), BF16),
            pltpu.VMEM((2, ROWS, 4 * S), F32),
            pltpu.VMEM((ROUNDS, 2, 4, 2, S, 2 * S), BF16),
            pltpu.VMEM((ROUNDS, NB * S, 2 * S), BF16),
            pltpu.VMEM((NB * S, NB * S), BF16),
            pltpu.VMEM((PL, NB * S, S), BF16),
            pltpu.VMEM((256, 256), BF16),
            dma((PL,)),
            dma((ROUNDS,)), dma((ROUNDS,)),
            dma(()), dma(()),
            dma(()), dma((2, NB)),
            dma(()), dma(()),
            dma((6,)), dma((4, 2)),
            dma(()), dma(()),
            dma((ROUNDS,)), dma((ROUNDS,)),
            dma(()),
        ],
        compiler_params=pltpu.CompilerParams(
            collective_id=0, has_side_effects=True, vmem_limit_bytes=56 << 20
        ),
        cost_estimate=pl.CostEstimate(flops=17 << 30, bytes_accessed=8 << 20, transcendentals=0),
    )(
        tensor.reshape(S, PL, NB, S), tensor_mask,
        occ_density.reshape(S, 2, S), occ_mask, virt_density.reshape(S, 2, S), virt_mask,
    )
    return jnp.transpose(out, (1, 0, 2)).reshape(NB, S, PL, 1, S)


def solution(mesh):
    placed = (
        P("wide", None, "narrow", None, None),
        P("wide", None),
        P("wide", None, "narrow", None),
        P("wide", "narrow"),
        P("wide", None, "narrow", None),
        P("wide", "narrow"),
    )
    return jax.shard_map(
        shards,
        mesh=mesh,
        in_specs=placed,
        out_specs=P(None, None, "narrow", "wide", None),
        check_vma=False,
    )
```

time: 229 us -> 112 us (0.49); the launches traced: 225 us -> 111 us
  waiting for transfers between devices: 140 us -> 0 us
  Pallas kernels: 0 us -> 104 us
  matrix products: 25.3 us -> 0 us
  local copies, waits for them, and re-layouts: 31.4 us -> 7.75 us
  between operations: 13.4 us -> 0.01 us
  other arithmetic: 9.58 us -> 0 us
  starting transfers between devices: 4.81 us -> 0 us
    all_gather x2 -> x0, waiting for transfers between devices: 140 us -> none  [the longest x1 72.2 us: shards(): lax.all_gather(virt_local[None], ('wide', 'narrow'), axis=0, tiled=True)]
    pallas_call x0 -> x1, Pallas kernels: none -> 104 us  [shards(): pl.pallas_call(kernel, out_shape=jax.ShapeDtypeStruct((PL, NB * S, S), BF...]
    dot_general x2 -> x0, matrix products: 25.3 us -> none  [the longest x1 12.7 us: shards(): jnp.dot(virt_full, remap_flat, preferred_element_type=jnp.float32)]
    reshape x3 -> x1, local copies, waits for them, and re-layouts: 28.3 us -> 7.75 us  [shards(): return jnp.transpose(out, (1, 0, 2)).reshape(NB, S, PL, 1, S)]
    mul x5 -> x0, other arithmetic: 5.04 us -> none  [the longest x2 2.19 us: shards(): occ_density * occ_mask.astype(occ_density.dtype)[:, None, :, None]]
    all_to_all x1 -> x0, starting transfers between devices: 4.76 us -> none  [shards(): lax.all_to_all(half_moved, 'wide', split_axis=3, concat_axis=0, tiled=True)]
    unnamed x1 -> x0, other arithmetic: 4.54 us -> none
    unnamed x1 -> x0, local copies, waits for them, and re-layouts: 3.1 us -> none
  transfers between devices with their start and end apart: 3 -> 0, of which waited for: 2 -> 0; matrix products, arithmetic and copies ran while one was open for 21% -> 0% of each run, Pallas kernels for 0% -> 0%
where the time goes in v1:
time: 112 us; the launch traced here: 111 us
  Pallas kernels  104 us (93%)
  local copies, waits for them, and re-layouts  7.75 us (7%)
    pallas_call x1, Pallas kernels, shards(): pl.pallas_call(kernel, out_shape=jax.ShapeDtypeStruct((PL, NB * S, S), BF...  104 us
    reshape x1, local copies, waits for them, and re-layouts, shards(): return jnp.transpose(out, (1, 0, 2)).reshape(NB, S, PL, 1, S)  7.75 us

profile of v1, /device:TPU:1, one launch (start us, length us, event | category | flops | bytes accessed | tf_op | source)
XLA Modules:
  0.0 111.4 jit_solution(7706843570965464097)
XLA Ops:
  0.0 103.7 %shard_map.64 = bf16[8,2048,128]{2,1,0:T(8,128)(2,1)} custom-call(bf16[128,8,16,128]{3,2,1,0:T(8,128)(2,1)} %bitcast.7, s32[1,16]{1,0:T(1,128)} %tmask.1, bf16[128,2,128]{2,1,0:T(2,128)(2,1)} %bitcast.8, s32[1,2]{1,0:T(1,128)} %omask.1, bf16[128,2,128]{2,1,0:T(2,128)(2,1)} %bitcast.9, s32[1,2]{1,0:T(1,128)} %vmask.1), custom_call_target="tpu_custom_call" | custom-call | flops 18253611008 | bytes 8388608 | tf_op jit(solution)/shard_map/pallas_call | solution.py:318
  103.7 7.7 %copy.7 = bf16[16,128,8,1,128]{4,2,3,1,0:T(8,128)(2,1)} copy(bf16[16,128,8,1,128]{4,1,0,2,3:T(8,128)(2,1)} %bitcast.6) | data formatting | bytes 8388608 | tf_op jit(solution)/shard_map/reshape | solution.py:351

commit v2 on v1

v2 whole, which is shorter than its diff:
```python
import functools

import jax
import jax.numpy as jnp
from jax import lax
from jax.experimental import pallas as pl
from jax.experimental.pallas import tpu as pltpu
from jax.sharding import PartitionSpec as P

MESH = pl.DeviceIdType.MESH
BF16 = jnp.bfloat16
F32 = jnp.float32
S = 128
NB = 16
PL = 8
ROUNDS = 4
ROWS = 2 * PL * S
NA = 80
NC = S - NA


NEAR = (
    (1, 0), (0, 1), (3, 0), (0, 3), (1, 1), (3, 3), (1, 3), (3, 1),
    (2, 0), (0, 2), (2, 1), (1, 2), (2, 3), (3, 2), (2, 2),
)


def ring(v):
    return lax.rem(v + 4, 4)


def kernel(
    t_hbm, tmask, occ_ref, omask, virt_ref, vmask, out_hbm,
    traw, tm, occ, send, recv, virt, stage, outv, perm,
    t_sem, x_ssem, x_rsem, o1_ssem, o1_rsem, o2_ssem, o3_ssem, o_rsem, c1_ssem, c1_rsem, c2_ssem, c2_rsem,
    v1_ssem, v1_rsem, v1b_ssem, v1b_rsem, v2_ssem, v2_rsem, v3_ssem, v3_rsem,
    a_ssem, a_rsem, out_sem,
):
    w = lax.axis_index("wide")
    n = lax.axis_index("narrow")
    x, z = w // 4, lax.rem(w, 4)
    y, k = n // 2, lax.rem(n, 2)

    def remote(src, dst, ssem, rsem, wide, narrow):
        return pltpu.make_async_remote_copy(
            src_ref=src, dst_ref=dst, send_sem=ssem, recv_sem=rsem,
            device_id=(wide, narrow), device_id_type=MESH,
        )

    def wait_kib(sem, kib):
        view = recv.at[0, pl.ds(0, kib * 2), :] if kib < 1024 else tm.at[pl.ds(0, kib // 4), :]
        pltpu.make_async_copy(view, view, sem).wait()

    barrier = pltpu.get_barrier_semaphore()
    for d in range(1, 4):
        pl.semaphore_signal(barrier, inc=1, device_id=(w, ring(y + d) * 2 + k), device_id_type=MESH)
    for d in range(1, 16):
        for e in range(2):
            pl.semaphore_signal(
                barrier, inc=1, device_id=(lax.rem(w + d, 16), y * 2 + e), device_id_type=MESH
            )
    pl.semaphore_signal(barrier, inc=1, device_id=(w, y * 2 + 1 - k), device_id_type=MESH)

    for p in range(PL):
        pltpu.make_async_copy(t_hbm.at[:, p], traw.at[p], t_sem.at[p]).start()

    ycol = pl.ds(pl.multiple_of(y * S, S), S)
    ncol = pl.ds(pl.multiple_of(n * 2 * S, 2 * S), 2 * S)
    wrow = pl.ds(pl.multiple_of(w * S, S), S)
    for j in range(2):
        block = occ_ref[:, j, :].astype(F32) * omask[0, j].astype(F32)
        occ[j, w, :, ycol] = block.astype(BF16)
    for j in range(2):
        block = virt_ref[:, j, :].astype(F32) * vmask[0, j].astype(F32)
        virt[x, z, :, pl.ds(pl.multiple_of(n * 2 * S + j * S, S), S)] = block.astype(BF16)

    row = lax.broadcasted_iota(jnp.int32, (256, 256), 0)
    col = lax.broadcasted_iota(jnp.int32, (256, 256), 1)
    scale = jnp.zeros((256, 256), F32)
    for b in range(NB):
        scale = scale + jnp.where((row >> 4) == b, 1.0, 0.0) * tmask[0, b].astype(F32)
    hit = jnp.logical_and((row >> 4) == (col & 15), (row & 15) == (col >> 4))
    perm[...] = jnp.where(hit, scale, 0.0).astype(BF16)

    pl.semaphore_wait(barrier, 34)

    first, other = pl.ds(0, NA), pl.ds(NA, NC)
    for d in (1, 3, 2):
        for i in range(2):
            own = occ.at[i, w, first, ycol]
            remote(own, own, o1_ssem, o1_rsem, w, ring(y + d) * 2 + k).start()
    for dx, dz in NEAR:
        own = occ.at[:, w, other, ycol]
        remote(own, own, c1_ssem, c1_rsem, ring(x + dx) * 4 + ring(z + dz), n).start()
    place = ((x, z), (z, x))

    def at(i, p, q):
        return p * 4 + q if i == 0 else q * 4 + p

    upper, lower = pl.ds(0, S // 2), pl.ds(S // 2, S // 2)
    for d in (1, 3, 2):
        for i, part in enumerate((upper, lower)):
            p, q = place[i]
            own = virt.at[x, z, part, ncol]
            remote(own, own, v1_ssem, v1_rsem, at(i, ring(p + d), q), n).start()

    def own_rows(r):
        return pl.ds(pl.multiple_of(r * 512 + k * 256, 256), 256)

    def relayout(r):
        for pi in range(2):
            p = 2 * r + pi
            pltpu.make_async_copy(t_hbm.at[:, p], traw.at[p], t_sem.at[p]).wait()

            def body(g, c, p=p, pi=pi):
                pair = jnp.concatenate(
                    [
                        traw[p, pl.ds(pl.multiple_of(g * 32 + h * 16, 16), 16)].reshape(256, S)
                        for h in range(2)
                    ],
                    axis=1,
                )
                got = jnp.dot(perm[...], pair, preferred_element_type=F32).astype(BF16)
                for h in range(2):
                    top = r * 512 + k * 256 + pi * S + g * 32 + h * 16
                    for b in range(NB):
                        tm[pl.ds(pl.multiple_of(top, 16), 16), b * S : (b + 1) * S] = got[
                            b * 16 : (b + 1) * 16, h * S : (h + 1) * S
                        ]
                return c

            lax.fori_loop(0, 4, body, 0)
        mine = tm.at[own_rows(r), :]
        remote(mine, mine, x_ssem.at[r], x_rsem.at[r], w, y * 2 + 1 - k).start()

    relayout(0)

    def pass_block(i, b, p, q, ssem=o3_ssem):
        part = occ.at[i, b, first, :]
        remote(part, part, ssem, o_rsem.at[i, b], at(i, p, q), n).start()

    def wait_block(i, b):
        part = occ.at[i, b, first, :]
        pltpu.make_async_copy(part, part, o_rsem.at[i, b]).wait()

    def spread(i, yy, d):
        part = occ.at[i, :, other, pl.ds(pl.multiple_of(yy * S, S), S)]
        remote(part, part, c2_ssem, c2_rsem.at[yy, i], w, ring(y + d) * 2 + k).start()

    def wait_spread(i, yy):
        part = occ.at[i, :, other, pl.ds(pl.multiple_of(yy * S, S), S)]
        pltpu.make_async_copy(part, part, c2_rsem.at[yy, i]).wait()

    up, down, far = ring(y + 1), ring(y + 3), ring(y + 2)

    wait_kib(o1_rsem, 6 * NA // 4)
    for d in (1, 3, 2):
        for i in range(2):
            p, q = place[i]
            pass_block(i, w, ring(p + d), q, o2_ssem)
    for i in range(2):
        p, q = place[i]
        for d in (1, 3):
            pass_block(i, w, p, ring(q + d))

    wait_kib(c1_rsem, 15 * NC // 2)
    for i, d in ((0, 3), (1, 1), (0, 1), (1, 3)):
        spread(i, y, d)

    wait_kib(v1_rsem, 192)
    for d in (1, 3, 2):
        for i, part in enumerate((virt.at[:, z, upper, ncol], virt.at[x, :, lower, ncol])):
            p, q = place[i]
            remote(part, part, v1b_ssem, v1b_rsem, at(i, p, ring(q + d)), n).start()

    relayout(1)
    for d in (1, 3, 2):
        for i in range(2):
            p, q = place[i]
            b = at(i, ring(p + d), q)
            wait_block(i, b)
            for f in (1, 3):
                pass_block(i, b, p, ring(q + f))
    relayout(2)
    wait_spread(0, up)
    spread(0, up, 3)
    wait_spread(1, down)
    spread(1, down, 1)
    for f, g in ((0, 3), (1, 2)):
        for i in range(2):
            p, q = place[i]
            for dq, dp, to in ((1, f, 3), (3, g, 1)):
                b = at(i, ring(p + dp), ring(q + dq))
                wait_block(i, b)
                pass_block(i, b, p, ring(q + to))
        if f == 0:
            relayout(3)

    halves = [pl.ds(0, 2), pl.ds(2, 2)]

    def columns(yy, kk):
        return pl.ds(pl.multiple_of((yy * 2 + kk) * 2 * S, 2 * S), 2 * S)

    def to_core(yy, h):
        part = virt.at[halves[h], :, :, columns(yy, k)]
        remote(part, part, v3_ssem, v3_rsem, w, y * 2 + 1 - k).start()

    def along(yy, h, d, s):
        part = virt.at[halves[h], :, :, columns(yy, k)]
        remote(part, part, v2_ssem.at[s], v2_rsem.at[lax.rem(yy, 4), h], w, ring(y + d) * 2 + k).start()

    def wait_along(yy, h):
        part = virt.at[halves[h], :, :, columns(yy, k)]
        pltpu.make_async_copy(part, part, v2_rsem.at[yy, h]).wait()

    wait_kib(v1b_rsem, 768)
    along(y, 0, 3, 0)
    along(y, 1, 1, 1)
    along(y, 1, 3, 2)
    along(y, 0, 1, 3)
    to_core(y, 0)
    to_core(y, 1)

    for r in range(ROUNDS):
        theirs = tm.at[pl.ds(pl.multiple_of(r * 512 + (1 - k) * 256, 256), 256), :]
        pltpu.make_async_copy(theirs, theirs, x_rsem.at[r]).wait()
    for i in range(2):
        p, q = place[i]
        for dq, dp in ((1, 3), (1, 2), (3, 0), (3, 1), (2, 0), (2, 1), (2, 2), (2, 3)):
            wait_block(i, at(i, ring(p + dp), ring(q + dq)))
        for yy in (far, up if i == 1 else down):
            wait_spread(i, yy)

    def first_product(r, c):
        for j in range(2):
            i = lax.rem(j + z, 2)
            for e in range(2):
                rows = pl.ds(pl.multiple_of(r * 512 + e * 256, 256), 256)
                got = jnp.dot(
                    tm[rows, :], occ[i].reshape(NB * S, 4 * S), preferred_element_type=F32
                ).astype(BF16)
                for xx in range(4):
                    for pi in range(2):
                        send[r, i, xx, e, :, pi * S : (pi + 1) * S] = got[
                            pi * S : (pi + 1) * S, xx * S : (xx + 1) * S
                        ]
            for d in (1, 3, 2, 0):
                xx = ring(x + d)
                for e in range(2):
                    wide = xx * 4 + 2 * k + i
                    here = jnp.logical_and(wide == w, k == e)
                    src = send.at[r, i, xx, e]
                    dst = recv.at[r, wrow, :]

                    def away(src=src, dst=dst, wide=wide, e=e):
                        remote(src, dst, a_ssem.at[r], a_rsem.at[r], wide, y * 2 + e).start()

                    if d == 0:
                        pl.when(jnp.logical_not(here))(away)

                        @pl.when(here)
                        def _(src=src, dst=dst):
                            pltpu.make_async_copy(src, dst, a_rsem.at[r]).start()
                    else:
                        away()
        return c

    lax.fori_loop(0, ROUNDS, first_product, 0)

    wait_along(up, 0)
    along(up, 0, 3, 4)
    to_core(up, 0)
    wait_along(down, 1)
    along(down, 1, 1, 5)
    to_core(down, 1)
    wait_along(up, 1)
    to_core(up, 1)
    wait_along(down, 0)
    to_core(down, 0)
    wait_along(far, 0)
    to_core(far, 0)
    wait_along(far, 1)
    to_core(far, 1)
    wait_kib(v3_rsem, 4096)

    def second(r, last):
        pltpu.make_async_copy(recv.at[r], recv.at[r], a_rsem.at[r]).wait()

        def chunk(m, c):
            rows = pl.ds(pl.multiple_of(m * 256, 256), 256)
            lhs = virt[m // 2, pl.ds(lax.rem(m, 2) * 2, 2)].reshape(256, NB * S)
            got = jnp.dot(lhs, recv[r], preferred_element_type=F32)
            for pi in range(2):
                stage[rows, 2 * r + pi, :] = got[:, pi * S : (pi + 1) * S]
            if last:
                outv[rows] = stage[rows].astype(BF16)
                pltpu.make_async_copy(outv.at[rows], out_hbm.at[rows], out_sem).start()
            return c

        lax.fori_loop(0, 8, chunk, 0)

    for r in range(ROUNDS):
        second(r, r == ROUNDS - 1)

    pltpu.make_async_copy(outv, out_hbm, out_sem).wait()
    wait_kib(o1_ssem, 6 * NA // 4)
    wait_kib(o2_ssem, 6 * NA)
    wait_kib(o3_ssem, 24 * NA)
    wait_kib(c1_ssem, 15 * NC // 2)
    wait_kib(c2_ssem, 24 * NC)
    wait_kib(v1_ssem, 192)
    wait_kib(v1b_ssem, 768)
    for t in range(6):
        wait_kib(v2_ssem.at[t], 512)
    wait_kib(v3_ssem, 4096)
    for r in range(ROUNDS):
        mine = tm.at[own_rows(r), :]
        pltpu.make_async_copy(mine, mine, x_ssem.at[r]).wait()
        local = z // 2 == k

        @pl.when(local)
        def _(r=r):
            wait_kib(a_ssem.at[r], 960)

        @pl.when(jnp.logical_not(local))
        def _(r=r):
            wait_kib(a_ssem.at[r], 1024)


def shards(tensor, tensor_mask, occ_density, occ_mask, virt_density, virt_mask):
    dma = pltpu.SemaphoreType.DMA
    vmem, smem = pl.BlockSpec(memory_space=pltpu.VMEM), pl.BlockSpec(memory_space=pltpu.SMEM)
    out = pl.pallas_call(
        kernel,
        out_shape=jax.ShapeDtypeStruct((NB * S, PL, S), BF16),
        in_specs=[pl.BlockSpec(memory_space=pl.ANY), smem, vmem, smem, vmem, smem],
        out_specs=pl.BlockSpec(memory_space=pl.ANY),
        scratch_shapes=[
            pltpu.VMEM((PL, S, NB, S), BF16),
            pltpu.VMEM((ROWS, NB * S), BF16),
            pltpu.VMEM((2, NB, S, 4 * S), BF16),
            pltpu.VMEM((ROUNDS, 2, 4, 2, S, 2 * S), BF16),
            pltpu.VMEM((ROUNDS, NB * S, 2 * S), BF16),
            pltpu.VMEM((4, 4, S, NB * S), BF16),
            pltpu.VMEM((NB * S, PL, S), F32),
            pltpu.VMEM((NB * S, PL, S), BF16),
            pltpu.VMEM((256, 256), BF16),
            dma((PL,)),
            dma((ROUNDS,)), dma((ROUNDS,)),
            dma(()), dma(()),
            dma(()), dma(()), dma((2, NB)),
            dma(()), dma(()), dma(()), dma((4, 2)),
            dma(()), dma(()),
            dma(()), dma(()),
            dma((6,)), dma((4, 2)),
            dma(()), dma(()),
            dma((ROUNDS,)), dma((ROUNDS,)),
            dma(()),
        ],
        compiler_params=pltpu.CompilerParams(
            collective_id=0, has_side_effects=True, vmem_limit_bytes=56 << 20
        ),
        cost_estimate=pl.CostEstimate(flops=17 << 30, bytes_accessed=8 << 20, transcendentals=0),
    )(
        tensor.reshape(S, PL, NB, S), tensor_mask,
        occ_density.reshape(S, 2, S), occ_mask, virt_density.reshape(S, 2, S), virt_mask,
    )
    return out.reshape(NB, S, PL, 1, S)


def solution(mesh):
    placed = (
        P("wide", None, "narrow", None, None),
        P("wide", None),
        P("wide", None, "narrow", None),
        P("wide", "narrow"),
        P("wide", None, "narrow", None),
        P("wide", "narrow"),
    )
    return jax.shard_map(
        shards,
        mesh=mesh,
        in_specs=placed,
        out_specs=P(None, None, "narrow", "wide", None),
        check_vma=False,
    )
```

time: 112 us -> 102 us (0.911)
  Pallas kernels: 104 us -> 97.3 us
  local copies, waits for them, and re-layouts: 7.75 us -> 4.61 us
    reshape x1 -> x0, local copies, waits for them, and re-layouts: 7.75 us -> none  [shards(): return jnp.transpose(out, (1, 0, 2)).reshape(NB, S, PL, 1, S)]
    pallas_call x1, Pallas kernels: 104 us -> 97.3 us  [shards(): pl.pallas_call(kernel, out_shape=jax.ShapeDtypeStruct((NB * S, PL, S), BF...]
    unnamed x0 -> x1, local copies, waits for them, and re-layouts: none -> 4.61 us
where the time goes in v2:
time: 102 us
  Pallas kernels  97.3 us (95%)
  local copies, waits for them, and re-layouts  4.61 us (5%)
    pallas_call x1, Pallas kernels, shards(): pl.pallas_call(kernel, out_shape=jax.ShapeDtypeStruct((NB * S, PL, S), BF...  97.3 us
    unnamed x1, local copies, waits for them, and re-layouts  4.61 us

profile of v2, /device:TPU:1, one launch (start us, length us, event | category | flops | bytes accessed | tf_op | source)
XLA Modules:
  0.0 101.9 jit_solution(6183636230118454032)
XLA Ops:
  0.0 97.3 %shard_map.64 = bf16[2048,8,128]{2,1,0:T(8,128)(2,1)} custom-call(bf16[128,8,16,128]{3,2,1,0:T(8,128)(2,1)} %bitcast.7, s32[1,16]{1,0:T(1,128)} %tmask.1, bf16[128,2,128]{2,1,0:T(2,128)(2,1)} %bitcast.8, s32[1,2]{1,0:T(1,128)} %omask.1, bf16[128,2,128]{2,1,0:T(2,128)(2,1)} %bitcast.9, s32[1,2]{1,0:T(1,128)} %vmask.1), custom_call_target="tpu_custom_call" | custom-call | flops 18253611008 | bytes 8388608 | tf_op jit(solution)/shard_map/pallas_call | solution.py:333
  97.3 4.6 %copy.9 = bf16[16,128,8,1,128]{4,2,3,1,0:T(8,128)(2,1)} copy(bf16[16,128,8,1,128]{4,2,3,1,0:T(8,128)(2,1)} %bitcast.6) | data formatting | bytes 8388608

commit v3 on v2

--- a/solution.py
+++ b/solution.py
@@ -17,6 +17,9 @@
 ROWS = 2 * PL * S
 NA = 80
 NC = S - NA
+VMEM_LIMIT = 43 << 20
+LAST_LIMIT = 8 << 20
+CHUNK = 512
 
 
 NEAR = (
@@ -29,12 +32,34 @@
     return lax.rem(v + 4, 4)
 
 
+def second_product(virt, recv, stage, r, m, c):
+    rows = pl.ds(pl.multiple_of(m * CHUNK, CHUNK), CHUNK)
+    per = CHUNK // S
+    lhs = virt[m * per // 4, pl.ds(lax.rem(m * per, 4), per)].reshape(CHUNK, NB * S)
+    got = jnp.dot(lhs, recv[r], preferred_element_type=F32)
+    for pi in range(2):
+        stage[rows, 2 * r + pi, :] = got[:, pi * S : (pi + 1) * S]
+    return c
+
+
+def last_kernel(virt, recv, stage, out_hbm, outv, out_sem):
+    def body(m, c):
+        second_product(virt, recv, stage, ROUNDS - 1, m, c)
+        rows = pl.ds(pl.multiple_of(m * CHUNK, CHUNK), CHUNK)
+        outv[rows] = stage[rows].astype(BF16)
+        pltpu.make_async_copy(outv.at[rows], out_hbm.at[rows], out_sem).start()
+        return c
+
+    lax.fori_loop(0, NB * S // CHUNK, body, 0)
+    pltpu.make_async_copy(outv, out_hbm, out_sem).wait()
+
+
 def kernel(
-    t_hbm, tmask, occ_ref, omask, virt_ref, vmask, out_hbm,
-    traw, tm, occ, send, recv, virt, stage, outv, perm,
+    t_hbm, tmask, occ_ref, omask, virt_ref, vmask, virt, recv, stage,
+    traw, tm, occ, send, perm,
     t_sem, x_ssem, x_rsem, o1_ssem, o1_rsem, o2_ssem, o3_ssem, o_rsem, c1_ssem, c1_rsem, c2_ssem, c2_rsem,
     v1_ssem, v1_rsem, v1b_ssem, v1b_rsem, v2_ssem, v2_rsem, v3_ssem, v3_rsem,
-    a_ssem, a_rsem, out_sem,
+    a_ssem, a_rsem,
 ):
     w = lax.axis_index("wide")
     n = lax.axis_index("narrow")
@@ -283,26 +308,11 @@
     to_core(far, 1)
     wait_kib(v3_rsem, 4096)
 
-    def second(r, last):
+    for r in range(ROUNDS):
         pltpu.make_async_copy(recv.at[r], recv.at[r], a_rsem.at[r]).wait()
-
-        def chunk(m, c):
-            rows = pl.ds(pl.multiple_of(m * 256, 256), 256)
-            lhs = virt[m // 2, pl.ds(lax.rem(m, 2) * 2, 2)].reshape(256, NB * S)
-            got = jnp.dot(lhs, recv[r], preferred_element_type=F32)
-            for pi in range(2):
-                stage[rows, 2 * r + pi, :] = got[:, pi * S : (pi + 1) * S]
-            if last:
-                outv[rows] = stage[rows].astype(BF16)
-                pltpu.make_async_copy(outv.at[rows], out_hbm.at[rows], out_sem).start()
-            return c
-
-        lax.fori_loop(0, 8, chunk, 0)
-
-    for r in range(ROUNDS):
-        second(r, r == ROUNDS - 1)
-
-    pltpu.make_async_copy(outv, out_hbm, out_sem).wait()
+        if r < ROUNDS - 1:
+            lax.fori_loop(0, NB * S // CHUNK, functools.partial(second_product, virt, recv, stage, r), 0)
+
     wait_kib(o1_ssem, 6 * NA // 4)
     wait_kib(o2_ssem, 6 * NA)
     wait_kib(o3_ssem, 24 * NA)
@@ -330,20 +340,20 @@
 def shards(tensor, tensor_mask, occ_density, occ_mask, virt_density, virt_mask):
     dma = pltpu.SemaphoreType.DMA
     vmem, smem = pl.BlockSpec(memory_space=pltpu.VMEM), pl.BlockSpec(memory_space=pltpu.SMEM)
-    out = pl.pallas_call(
+    virt, recv, stage = pl.pallas_call(
         kernel,
-        out_shape=jax.ShapeDtypeStruct((NB * S, PL, S), BF16),
+        out_shape=[
+            pltpu.VMEM((4, 4, S, NB * S), BF16),
+            pltpu.VMEM((ROUNDS, NB * S, 2 * S), BF16),
+            pltpu.VMEM((NB * S, PL, S), F32),
+        ],
         in_specs=[pl.BlockSpec(memory_space=pl.ANY), smem, vmem, smem, vmem, smem],
-        out_specs=pl.BlockSpec(memory_space=pl.ANY),
+        out_specs=[vmem] * 3,
         scratch_shapes=[
             pltpu.VMEM((PL, S, NB, S), BF16),
             pltpu.VMEM((ROWS, NB * S), BF16),
             pltpu.VMEM((2, NB, S, 4 * S), BF16),
             pltpu.VMEM((ROUNDS, 2, 4, 2, S, 2 * S), BF16),
-            pltpu.VMEM((ROUNDS, NB * S, 2 * S), BF16),
-            pltpu.VMEM((4, 4, S, NB * S), BF16),
-            pltpu.VMEM((NB * S, PL, S), F32),
-            pltpu.VMEM((NB * S, PL, S), BF16),
             pltpu.VMEM((256, 256), BF16),
             dma((PL,)),
             dma((ROUNDS,)), dma((ROUNDS,)),
@@ -355,16 +365,24 @@
             dma((6,)), dma((4, 2)),
             dma(()), dma(()),
             dma((ROUNDS,)), dma((ROUNDS,)),
-            dma(()),
         ],
         compiler_params=pltpu.CompilerParams(
-            collective_id=0, has_side_effects=True, vmem_limit_bytes=56 << 20
+            collective_id=0, has_side_effects=True, vmem_limit_bytes=VMEM_LIMIT
         ),
-        cost_estimate=pl.CostEstimate(flops=17 << 30, bytes_accessed=8 << 20, transcendentals=0),
+        cost_estimate=pl.CostEstimate(flops=15 << 30, bytes_accessed=8 << 20, transcendentals=0),
     )(
         tensor.reshape(S, PL, NB, S), tensor_mask,
         occ_density.reshape(S, 2, S), occ_mask, virt_density.reshape(S, 2, S), virt_mask,
     )
+    out = pl.pallas_call(
+        last_kernel,
+        out_shape=jax.ShapeDtypeStruct((NB * S, PL, S), BF16),
+        in_specs=[vmem] * 3,
+        out_specs=pl.BlockSpec(memory_space=pl.ANY),
+        scratch_shapes=[pltpu.VMEM((NB * S, PL, S), BF16), dma(())],
+        compiler_params=pltpu.CompilerParams(vmem_limit_bytes=LAST_LIMIT),
+        cost_estimate=pl.CostEstimate(flops=2 << 30, bytes_accessed=4 << 20, transcendentals=0),
+    )(virt, recv, stage)
     return out.reshape(NB, S, PL, 1, S)
 
 

time: 102 us -> 96.8 us (0.949)
  local copies, waits for them, and re-layouts: 4.61 us -> 0 us
    unnamed x1 -> x0, local copies, waits for them, and re-layouts: 4.61 us -> none
    pallas_call x1 -> x2, Pallas kernels: 97.3 us -> 96.7 us  [the longest x1 91.5 us: shards(): pl.pallas_call(kernel, out_shape=[pltpu.VMEM((4, 4, S, NB * S), BF16), pl...]
where the time goes in v3:
time: 96.8 us; the launch traced here: 96.7 us
  Pallas kernels  96.7 us (100%)
    pallas_call x1, Pallas kernels, shards(): pl.pallas_call(kernel, out_shape=[pltpu.VMEM((4, 4, S, NB * S), BF16), pl...  91.5 us
    pallas_call x1, Pallas kernels, shards(): pl.pallas_call(last_kernel, out_shape=jax.ShapeDtypeStruct((NB * S, PL, S...  5.21 us

profile of v3, /device:TPU:1, one launch (start us, length us, event | category | flops | bytes accessed | tf_op | source)
XLA Modules:
  0.0 96.7 jit_solution(16717829419081917300)
XLA Ops:
  0.0 91.5 %shard_map.64 = (bf16[4,4,128,2048]{3,2,1,0:T(8,128)(2,1)S(1)}, bf16[4,2048,256]{2,1,0:T(8,128)(2,1)S(1)}, f32[2048,8,128]{2,1,0:T(8,128)S(1)}) custom-call(bf16[128,8,16,128]{3,2,1,0:T(8,128)(2,1)} %bitcast.6, s32[1,16]{1,0:T(1,128)} %tmask.1, bf16[128,2,128]{2,1,0:T(2,128)(2,1)} %bitcast.7, s32[1,2]{1,0:T(1,128)} %omask.1, bf16[128,2,128]{2,1,0:T(2,128)(2,1)} %bitcast.8, ...), custom_call_target="tpu_custom_call" | custom-call | flops 16106127360 | bytes 8388608 | tf_op jit(solution)/shard_map/pallas_call | solution.py:343
  91.5 5.2 %shard_map.65 = bf16[2048,8,128]{2,1,0:T(8,128)(2,1)} custom-call(bf16[4,4,128,2048]{3,2,1,0:T(8,128)(2,1)S(1)} %get-tuple-element.8.virt, bf16[4,2048,256]{2,1,0:T(8,128)(2,1)S(1)} %get-tuple-element.9.recv, f32[2048,8,128]{2,1,0:T(8,128)S(1)} %get-tuple-element.10.stage), custom_call_target="tpu_custom_call" | custom-call | flops 2147483648 | bytes 4194304 | tf_op jit(solution)/shard_map/pallas_call | solution.py:377

commit v4 on v3

--- a/solution.py
+++ b/solution.py
@@ -17,9 +17,10 @@
 ROWS = 2 * PL * S
 NA = 80
 NC = S - NA
-VMEM_LIMIT = 43 << 20
+VMEM_LIMIT = 47 << 20
 LAST_LIMIT = 8 << 20
-CHUNK = 512
+CHUNK = 4 * S
+HALF = NB * S // 2
 
 
 NEAR = (
@@ -32,21 +33,20 @@
     return lax.rem(v + 4, 4)
 
 
-def second_product(virt, recv, stage, r, m, c):
-    rows = pl.ds(pl.multiple_of(m * CHUNK, CHUNK), CHUNK)
-    per = CHUNK // S
-    lhs = virt[m * per // 4, pl.ds(lax.rem(m * per, 4), per)].reshape(CHUNK, NB * S)
-    got = jnp.dot(lhs, recv[r], preferred_element_type=F32)
-    for pi in range(2):
-        stage[rows, 2 * r + pi, :] = got[:, pi * S : (pi + 1) * S]
-    return c
-
-
-def last_kernel(virt, recv, stage, out_hbm, outv, out_sem):
+def chunk_rows(m):
+    return pl.ds(pl.multiple_of(m * CHUNK, CHUNK), CHUNK)
+
+
+def product(virt, recv, r, m):
+    lhs = virt[m].reshape(CHUNK, NB * S)
+    return jnp.dot(lhs, recv[r], preferred_element_type=F32).astype(BF16).reshape(CHUNK, 2, S)
+
+
+def last_kernel(virt, recv, done, out_hbm, outv, out_sem):
     def body(m, c):
-        second_product(virt, recv, stage, ROUNDS - 1, m, c)
-        rows = pl.ds(pl.multiple_of(m * CHUNK, CHUNK), CHUNK)
-        outv[rows] = stage[rows].astype(BF16)
+        rows = chunk_rows(m)
+        outv[rows] = done[rows]
+        outv[rows, PL - 2 : PL, :] = product(virt, recv, ROUNDS - 1, m)
         pltpu.make_async_copy(outv.at[rows], out_hbm.at[rows], out_sem).start()
         return c
 
@@ -55,8 +55,8 @@
 
 
 def kernel(
-    t_hbm, tmask, occ_ref, omask, virt_ref, vmask, virt, recv, stage,
-    traw, tm, occ, send, perm,
+    t_hbm, tmask_hbm, occ_hbm, omask_hbm, virt_hbm, vmask_hbm, virt, recv, done,
+    tmask, occ_ref, omask, virt_ref, vmask, in_sem, traw, tm, occ, send, perm,
     t_sem, x_ssem, x_rsem, o1_ssem, o1_rsem, o2_ssem, o3_ssem, o_rsem, c1_ssem, c1_rsem, c2_ssem, c2_rsem,
     v1_ssem, v1_rsem, v1b_ssem, v1b_rsem, v2_ssem, v2_rsem, v3_ssem, v3_rsem,
     a_ssem, a_rsem,
@@ -77,17 +77,33 @@
         pltpu.make_async_copy(view, view, sem).wait()
 
     barrier = pltpu.get_barrier_semaphore()
-    for d in range(1, 4):
-        pl.semaphore_signal(barrier, inc=1, device_id=(w, ring(y + d) * 2 + k), device_id_type=MESH)
-    for d in range(1, 16):
+    for dx, dz in reversed(NEAR):
         for e in range(2):
             pl.semaphore_signal(
-                barrier, inc=1, device_id=(lax.rem(w + d, 16), y * 2 + e), device_id_type=MESH
+                barrier,
+                inc=1,
+                device_id=(ring(x + dx) * 4 + ring(z + dz), y * 2 + e),
+                device_id_type=MESH,
             )
+    for d in (2, 1, 3):
+        pl.semaphore_signal(barrier, inc=1, device_id=(w, ring(y + d) * 2 + k), device_id_type=MESH)
     pl.semaphore_signal(barrier, inc=1, device_id=(w, y * 2 + 1 - k), device_id_type=MESH)
 
+    inputs = [
+        pltpu.make_async_copy(src, dst, in_sem.at[t])
+        for t, (src, dst) in enumerate(
+            (
+                (omask_hbm, omask), (occ_hbm, occ_ref), (vmask_hbm, vmask),
+                (virt_hbm, virt_ref), (tmask_hbm, tmask),
+            )
+        )
+    ]
+    for copy in inputs:
+        copy.start()
     for p in range(PL):
         pltpu.make_async_copy(t_hbm.at[:, p], traw.at[p], t_sem.at[p]).start()
+    inputs[0].wait()
+    inputs[1].wait()
 
     ycol = pl.ds(pl.multiple_of(y * S, S), S)
     ncol = pl.ds(pl.multiple_of(n * 2 * S, 2 * S), 2 * S)
@@ -95,18 +111,6 @@
     for j in range(2):
         block = occ_ref[:, j, :].astype(F32) * omask[0, j].astype(F32)
         occ[j, w, :, ycol] = block.astype(BF16)
-    for j in range(2):
-        block = virt_ref[:, j, :].astype(F32) * vmask[0, j].astype(F32)
-        virt[x, z, :, pl.ds(pl.multiple_of(n * 2 * S + j * S, S), S)] = block.astype(BF16)
-
-    row = lax.broadcasted_iota(jnp.int32, (256, 256), 0)
-    col = lax.broadcasted_iota(jnp.int32, (256, 256), 1)
-    scale = jnp.zeros((256, 256), F32)
-    for b in range(NB):
-        scale = scale + jnp.where((row >> 4) == b, 1.0, 0.0) * tmask[0, b].astype(F32)
-    hit = jnp.logical_and((row >> 4) == (col & 15), (row & 15) == (col >> 4))
-    perm[...] = jnp.where(hit, scale, 0.0).astype(BF16)
-
     pl.semaphore_wait(barrier, 34)
 
     first, other = pl.ds(0, NA), pl.ds(NA, NC)
@@ -117,6 +121,12 @@
     for dx, dz in NEAR:
         own = occ.at[:, w, other, ycol]
         remote(own, own, c1_ssem, c1_rsem, ring(x + dx) * 4 + ring(z + dz), n).start()
+    inputs[2].wait()
+    inputs[3].wait()
+    for j in range(2):
+        block = virt_ref[:, j, :].astype(F32) * vmask[0, j].astype(F32)
+        virt[x, z, :, pl.ds(pl.multiple_of(n * 2 * S + j * S, S), S)] = block.astype(BF16)
+
     place = ((x, z), (z, x))
 
     def at(i, p, q):
@@ -128,6 +138,15 @@
             p, q = place[i]
             own = virt.at[x, z, part, ncol]
             remote(own, own, v1_ssem, v1_rsem, at(i, ring(p + d), q), n).start()
+
+    inputs[4].wait()
+    row = lax.broadcasted_iota(jnp.int32, (256, 256), 0)
+    col = lax.broadcasted_iota(jnp.int32, (256, 256), 1)
+    scale = jnp.zeros((256, 256), F32)
+    for b in range(NB):
+        scale = scale + jnp.where((row >> 4) == b, 1.0, 0.0) * tmask[0, b].astype(F32)
+    hit = jnp.logical_and((row >> 4) == (col & 15), (row & 15) == (col >> 4))
+    perm[...] = jnp.where(hit, scale, 0.0).astype(BF16)
 
     def own_rows(r):
         return pl.ds(pl.multiple_of(r * 512 + k * 256, 256), 256)
@@ -192,12 +211,6 @@
     for i, d in ((0, 3), (1, 1), (0, 1), (1, 3)):
         spread(i, y, d)
 
-    wait_kib(v1_rsem, 192)
-    for d in (1, 3, 2):
-        for i, part in enumerate((virt.at[:, z, upper, ncol], virt.at[x, :, lower, ncol])):
-            p, q = place[i]
-            remote(part, part, v1b_ssem, v1b_rsem, at(i, p, ring(q + d)), n).start()
-
     relayout(1)
     for d in (1, 3, 2):
         for i in range(2):
@@ -206,7 +219,25 @@
             wait_block(i, b)
             for f in (1, 3):
                 pass_block(i, b, p, ring(q + f))
-    relayout(2)
+    def line(i, q, h=None):
+        part = pl.ds(0, 4) if h is None else pl.ds(2 * h, 2)
+        return virt.at[part, q, upper, ncol] if i == 0 else virt.at[q, part, lower, ncol]
+
+    def pass_line(i, q, d, t, h=None):
+        ref = line(i, q, h)
+        p, here = place[i]
+        remote(ref, ref, v1b_ssem, v1b_rsem.at[i, t], at(i, p, ring(here + d)), n).start()
+
+    def wait_line(i, q, t, h=None):
+        ref = line(i, q, h)
+        pltpu.make_async_copy(ref, ref, v1b_rsem.at[i, t]).wait()
+
+    wait_kib(v1_rsem, 192)
+    for i in range(2):
+        q = place[i][1]
+        pass_line(i, q, 3, 0)
+        pass_line(i, q, 1, 1)
+
     wait_spread(0, up)
     spread(0, up, 3)
     wait_spread(1, down)
@@ -218,8 +249,6 @@
                 b = at(i, ring(p + dp), ring(q + dq))
                 wait_block(i, b)
                 pass_block(i, b, p, ring(q + to))
-        if f == 0:
-            relayout(3)
 
     halves = [pl.ds(0, 2), pl.ds(2, 2)]
 
@@ -238,17 +267,14 @@
         part = virt.at[halves[h], :, :, columns(yy, k)]
         pltpu.make_async_copy(part, part, v2_rsem.at[yy, h]).wait()
 
-    wait_kib(v1b_rsem, 768)
-    along(y, 0, 3, 0)
-    along(y, 1, 1, 1)
-    along(y, 1, 3, 2)
-    along(y, 0, 1, 3)
-    to_core(y, 0)
-    to_core(y, 1)
-
-    for r in range(ROUNDS):
-        theirs = tm.at[pl.ds(pl.multiple_of(r * 512 + (1 - k) * 256, 256), 256), :]
-        pltpu.make_async_copy(theirs, theirs, x_rsem.at[r]).wait()
+    for i in range(2):
+        q = place[i][1]
+        wait_line(i, ring(q + 1), 0)
+        pass_line(i, ring(q + 1), 3, 2, 0)
+        wait_line(i, ring(q + 3), 1)
+        pass_line(i, ring(q + 3), 1, 3, 1)
+    relayout(2)
+    relayout(3)
     for i in range(2):
         p, q = place[i]
         for dq, dp in ((1, 3), (1, 2), (3, 0), (3, 1), (2, 0), (2, 1), (2, 2), (2, 3)):
@@ -257,8 +283,10 @@
             wait_spread(i, yy)
 
     def first_product(r, c):
+        theirs = tm.at[pl.ds(pl.multiple_of(r * 512 + (1 - k) * 256, 256), 256), :]
+        pltpu.make_async_copy(theirs, theirs, x_rsem.at[r]).wait()
         for j in range(2):
-            i = lax.rem(j + z, 2)
+            i = lax.rem(j + x // 2, 2)
             for e in range(2):
                 rows = pl.ds(pl.multiple_of(r * 512 + e * 256, 256), 256)
                 got = jnp.dot(
@@ -269,28 +297,40 @@
                         send[r, i, xx, e, :, pi * S : (pi + 1) * S] = got[
                             pi * S : (pi + 1) * S, xx * S : (xx + 1) * S
                         ]
-            for d in (1, 3, 2, 0):
-                xx = ring(x + d)
-                for e in range(2):
+                for d in (1, 3, 2, 0):
+                    xx = ring(x + d)
                     wide = xx * 4 + 2 * k + i
                     here = jnp.logical_and(wide == w, k == e)
                     src = send.at[r, i, xx, e]
                     dst = recv.at[r, wrow, :]
-
-                    def away(src=src, dst=dst, wide=wide, e=e):
-                        remote(src, dst, a_ssem.at[r], a_rsem.at[r], wide, y * 2 + e).start()
+                    rsem = a_rsem.at[r, x // 2]
+
+                    def away(src=src, dst=dst, rsem=rsem, wide=wide, e=e):
+                        remote(src, dst, a_ssem.at[r], rsem, wide, y * 2 + e).start()
 
                     if d == 0:
                         pl.when(jnp.logical_not(here))(away)
 
                         @pl.when(here)
-                        def _(src=src, dst=dst):
-                            pltpu.make_async_copy(src, dst, a_rsem.at[r]).start()
+                        def _(src=src, dst=dst, rsem=rsem):
+                            pltpu.make_async_copy(src, dst, rsem).start()
                     else:
                         away()
         return c
 
-    lax.fori_loop(0, ROUNDS, first_product, 0)
+    first_product(0, 0)
+    for i in range(2):
+        q = place[i][1]
+        for h in range(2):
+            wait_line(i, ring(q + 2), 2 + h, h)
+    along(y, 0, 3, 0)
+    along(y, 1, 1, 1)
+    along(y, 1, 3, 2)
+    along(y, 0, 1, 3)
+    to_core(y, 0)
+    to_core(y, 1)
+
+    lax.fori_loop(1, ROUNDS, first_product, 0)
 
     wait_along(up, 0)
     along(up, 0, 3, 4)
@@ -308,10 +348,30 @@
     to_core(far, 1)
     wait_kib(v3_rsem, 4096)
 
-    for r in range(ROUNDS):
-        pltpu.make_async_copy(recv.at[r], recv.at[r], a_rsem.at[r]).wait()
-        if r < ROUNDS - 1:
-            lax.fori_loop(0, NB * S // CHUNK, functools.partial(second_product, virt, recv, stage, r), 0)
+    def arrive(r, h):
+        half = recv.at[r, pl.ds(pl.multiple_of(h * HALF, HALF), HALF), :]
+        pltpu.make_async_copy(half, half, a_rsem.at[r, h]).wait()
+
+    for r in range(ROUNDS - 1):
+        arrive(r, 0)
+        arrive(r, 1)
+
+        def second_product(m, c, r=r):
+            done[chunk_rows(m), 2 * r : 2 * r + 2, :] = product(virt, recv, r, m)
+            return c
+
+        lax.fori_loop(0, NB * S // CHUNK, second_product, 0)
+
+    def wait_sent(r):
+        local = z // 2 == k
+
+        @pl.when(local)
+        def _():
+            wait_kib(a_ssem.at[r], 960)
+
+        @pl.when(jnp.logical_not(local))
+        def _():
+            wait_kib(a_ssem.at[r], 1024)
 
     wait_kib(o1_ssem, 6 * NA // 4)
     wait_kib(o2_ssem, 6 * NA)
@@ -326,30 +386,33 @@
     for r in range(ROUNDS):
         mine = tm.at[own_rows(r), :]
         pltpu.make_async_copy(mine, mine, x_ssem.at[r]).wait()
-        local = z // 2 == k
-
-        @pl.when(local)
-        def _(r=r):
-            wait_kib(a_ssem.at[r], 960)
-
-        @pl.when(jnp.logical_not(local))
-        def _(r=r):
-            wait_kib(a_ssem.at[r], 1024)
+        if r < ROUNDS - 1:
+            wait_sent(r)
+
+    arrive(ROUNDS - 1, 0)
+    arrive(ROUNDS - 1, 1)
+    wait_sent(ROUNDS - 1)
 
 
 def shards(tensor, tensor_mask, occ_density, occ_mask, virt_density, virt_mask):
     dma = pltpu.SemaphoreType.DMA
-    vmem, smem = pl.BlockSpec(memory_space=pltpu.VMEM), pl.BlockSpec(memory_space=pltpu.SMEM)
-    virt, recv, stage = pl.pallas_call(
+    vmem, hbm = pl.BlockSpec(memory_space=pltpu.VMEM), pl.BlockSpec(memory_space=pl.ANY)
+    virt, recv, done = pl.pallas_call(
         kernel,
         out_shape=[
             pltpu.VMEM((4, 4, S, NB * S), BF16),
             pltpu.VMEM((ROUNDS, NB * S, 2 * S), BF16),
-            pltpu.VMEM((NB * S, PL, S), F32),
+            pltpu.VMEM((NB * S, PL, S), BF16),
         ],
-        in_specs=[pl.BlockSpec(memory_space=pl.ANY), smem, vmem, smem, vmem, smem],
+        in_specs=[hbm] * 6,
         out_specs=[vmem] * 3,
         scratch_shapes=[
+            pltpu.SMEM((1, NB), jnp.int32),
+            pltpu.VMEM((S, 2, S), BF16),
+            pltpu.SMEM((1, 2), jnp.int32),
+            pltpu.VMEM((S, 2, S), BF16),
+            pltpu.SMEM((1, 2), jnp.int32),
+            dma((5,)),
             pltpu.VMEM((PL, S, NB, S), BF16),
             pltpu.VMEM((ROWS, NB * S), BF16),
             pltpu.VMEM((2, NB, S, 4 * S), BF16),
@@ -361,10 +424,10 @@
             dma(()), dma(()), dma((2, NB)),
             dma(()), dma(()), dma(()), dma((4, 2)),
             dma(()), dma(()),
-            dma(()), dma(()),
+            dma(()), dma((2, 4)),
             dma((6,)), dma((4, 2)),
             dma(()), dma(()),
-            dma((ROUNDS,)), dma((ROUNDS,)),
+            dma((ROUNDS,)), dma((ROUNDS, 2)),
         ],
         compiler_params=pltpu.CompilerParams(
             collective_id=0, has_side_effects=True, vmem_limit_bytes=VMEM_LIMIT
@@ -382,7 +445,7 @@
         scratch_shapes=[pltpu.VMEM((NB * S, PL, S), BF16), dma(())],
         compiler_params=pltpu.CompilerParams(vmem_limit_bytes=LAST_LIMIT),
         cost_estimate=pl.CostEstimate(flops=2 << 30, bytes_accessed=4 << 20, transcendentals=0),
-    )(virt, recv, stage)
+    )(virt, recv, done)
     return out.reshape(NB, S, PL, 1, S)
 
 

time: 96.8 us -> 90.9 us (0.939); the launches traced: 96.7 us -> 89.7 us
  Pallas kernels: 96.7 us -> 89.7 us
    pallas_call x1, Pallas kernels: 91.5 us -> 85.3 us  [shards(): pl.pallas_call(kernel, out_shape=[pltpu.VMEM((4, 4, S, NB * S), BF16), pl...]
where the time goes in v4:
time: 90.9 us; the launch traced here: 89.7 us
  Pallas kernels  89.7 us (99%)
    pallas_call x1, Pallas kernels, shards(): pl.pallas_call(kernel, out_shape=[pltpu.VMEM((4, 4, S, NB * S), BF16), pl...  85.3 us
    pallas_call x1, Pallas kernels, shards(): pl.pallas_call(last_kernel, out_shape=jax.ShapeDtypeStruct((NB * S, PL, S...  4.44 us

profile of v4, /device:TPU:1, one launch (start us, length us, event | category | flops | bytes accessed | tf_op | source)
XLA Modules:
  0.0 89.7 jit_solution(5470297486707656692)
XLA Ops:
  0.0 85.3 %shard_map.64 = (bf16[4,4,128,2048]{3,2,1,0:T(8,128)(2,1)S(1)}, bf16[4,2048,256]{2,1,0:T(8,128)(2,1)S(1)}, bf16[2048,8,128]{2,1,0:T(8,128)(2,1)S(1)}) custom-call(bf16[128,8,16,128]{3,2,1,0:T(8,128)(2,1)} %bitcast.6, s32[1,16]{1,0:T(1,128)} %tmask_hbm.1, bf16[128,2,128]{2,1,0:T(2,128)(2,1)} %bitcast.7, s32[1,2]{1,0:T(1,128)} %omask_hbm.1, ...), custom_call_target="tpu_custom_call" | custom-call | flops 16106127360 | bytes 8388608 | tf_op jit(solution)/shard_map/pallas_call | solution.py:400
  85.3 4.4 %shard_map.65 = bf16[2048,8,128]{2,1,0:T(8,128)(2,1)} custom-call(bf16[4,4,128,2048]{3,2,1,0:T(8,128)(2,1)S(1)} %get-tuple-element.8.virt, bf16[4,2048,256]{2,1,0:T(8,128)(2,1)S(1)} %get-tuple-element.9.recv, bf16[2048,8,128]{2,1,0:T(8,128)(2,1)S(1)} %get-tuple-element.10.done), custom_call_target="tpu_custom_call" | custom-call | flops 2147483648 | bytes 4194304 | tf_op jit(solution)/shard_map/pallas_call | solution.py:440

commit v5 on v4

--- a/solution.py
+++ b/solution.py
@@ -19,6 +19,7 @@
 NC = S - NA
 VMEM_LIMIT = 47 << 20
 LAST_LIMIT = 8 << 20
+AHEAD = 2
 CHUNK = 4 * S
 HALF = NB * S // 2
 
@@ -56,7 +57,7 @@
 
 def kernel(
     t_hbm, tmask_hbm, occ_hbm, omask_hbm, virt_hbm, vmask_hbm, virt, recv, done,
-    tmask, occ_ref, omask, virt_ref, vmask, in_sem, traw, tm, occ, send, perm,
+    tmask, occ_ref, omask, virt_ref, vmask, in_sem, traw, tm, occ, send, perm, early,
     t_sem, x_ssem, x_rsem, o1_ssem, o1_rsem, o2_ssem, o3_ssem, o_rsem, c1_ssem, c1_rsem, c2_ssem, c2_rsem,
     v1_ssem, v1_rsem, v1b_ssem, v1b_rsem, v2_ssem, v2_rsem, v3_ssem, v3_rsem,
     a_ssem, a_rsem,
@@ -121,33 +122,12 @@
     for dx, dz in NEAR:
         own = occ.at[:, w, other, ycol]
         remote(own, own, c1_ssem, c1_rsem, ring(x + dx) * 4 + ring(z + dz), n).start()
-    inputs[2].wait()
-    inputs[3].wait()
-    for j in range(2):
-        block = virt_ref[:, j, :].astype(F32) * vmask[0, j].astype(F32)
-        virt[x, z, :, pl.ds(pl.multiple_of(n * 2 * S + j * S, S), S)] = block.astype(BF16)
-
     place = ((x, z), (z, x))
 
     def at(i, p, q):
         return p * 4 + q if i == 0 else q * 4 + p
 
     upper, lower = pl.ds(0, S // 2), pl.ds(S // 2, S // 2)
-    for d in (1, 3, 2):
-        for i, part in enumerate((upper, lower)):
-            p, q = place[i]
-            own = virt.at[x, z, part, ncol]
-            remote(own, own, v1_ssem, v1_rsem, at(i, ring(p + d), q), n).start()
-
-    inputs[4].wait()
-    row = lax.broadcasted_iota(jnp.int32, (256, 256), 0)
-    col = lax.broadcasted_iota(jnp.int32, (256, 256), 1)
-    scale = jnp.zeros((256, 256), F32)
-    for b in range(NB):
-        scale = scale + jnp.where((row >> 4) == b, 1.0, 0.0) * tmask[0, b].astype(F32)
-    hit = jnp.logical_and((row >> 4) == (col & 15), (row & 15) == (col >> 4))
-    perm[...] = jnp.where(hit, scale, 0.0).astype(BF16)
-
     def own_rows(r):
         return pl.ds(pl.multiple_of(r * 512 + k * 256, 256), 256)
 
@@ -177,8 +157,6 @@
         mine = tm.at[own_rows(r), :]
         remote(mine, mine, x_ssem.at[r], x_rsem.at[r], w, y * 2 + 1 - k).start()
 
-    relayout(0)
-
     def pass_block(i, b, p, q, ssem=o3_ssem):
         part = occ.at[i, b, first, :]
         remote(part, part, ssem, o_rsem.at[i, b], at(i, p, q), n).start()
@@ -210,8 +188,27 @@
     wait_kib(c1_rsem, 15 * NC // 2)
     for i, d in ((0, 3), (1, 1), (0, 1), (1, 3)):
         spread(i, y, d)
-
-    relayout(1)
+    inputs[2].wait()
+    inputs[3].wait()
+    for j in range(2):
+        block = virt_ref[:, j, :].astype(F32) * vmask[0, j].astype(F32)
+        virt[x, z, :, pl.ds(pl.multiple_of(n * 2 * S + j * S, S), S)] = block.astype(BF16)
+    for d in (1, 3, 2):
+        for i, part in enumerate((upper, lower)):
+            p, q = place[i]
+            own = virt.at[x, z, part, ncol]
+            remote(own, own, v1_ssem, v1_rsem, at(i, ring(p + d), q), n).start()
+
+    inputs[4].wait()
+    row = lax.broadcasted_iota(jnp.int32, (256, 256), 0)
+    col = lax.broadcasted_iota(jnp.int32, (256, 256), 1)
+    scale = jnp.zeros((256, 256), F32)
+    for b in range(NB):
+        scale = scale + jnp.where((row >> 4) == b, 1.0, 0.0) * tmask[0, b].astype(F32)
+    hit = jnp.logical_and((row >> 4) == (col & 15), (row & 15) == (col >> 4))
+    perm[...] = jnp.where(hit, scale, 0.0).astype(BF16)
+
+    relayout(0)
     for d in (1, 3, 2):
         for i in range(2):
             p, q = place[i]
@@ -238,6 +235,7 @@
         pass_line(i, q, 3, 0)
         pass_line(i, q, 1, 1)
 
+    relayout(1)
     wait_spread(0, up)
     spread(0, up, 3)
     wait_spread(1, down)
@@ -255,9 +253,9 @@
     def columns(yy, kk):
         return pl.ds(pl.multiple_of((yy * 2 + kk) * 2 * S, 2 * S), 2 * S)
 
-    def to_core(yy, h):
+    def to_core(yy, h, t=0):
         part = virt.at[halves[h], :, :, columns(yy, k)]
-        remote(part, part, v3_ssem, v3_rsem, w, y * 2 + 1 - k).start()
+        remote(part, part, v3_ssem, v3_rsem.at[t], w, y * 2 + 1 - k).start()
 
     def along(yy, h, d, s):
         part = virt.at[halves[h], :, :, columns(yy, k)]
@@ -342,22 +340,44 @@
     to_core(up, 1)
     wait_along(down, 0)
     to_core(down, 0)
-    wait_along(far, 0)
-    to_core(far, 0)
-    wait_along(far, 1)
-    to_core(far, 1)
-    wait_kib(v3_rsem, 4096)
-
     def arrive(r, h):
         half = recv.at[r, pl.ds(pl.multiple_of(h * HALF, HALF), HALF), :]
         pltpu.make_async_copy(half, half, a_rsem.at[r, h]).wait()
 
-    for r in range(ROUNDS - 1):
+    def some(r, m, planes):
+        cols = [pl.ds(pl.multiple_of(yy * 4 * S, 4 * S), 4 * S) for yy in planes]
+        lhs = jnp.concatenate([virt[m, :, :, c].reshape(CHUNK, 4 * S) for c in cols], axis=1)
+        rhs = jnp.concatenate([recv[r, c, :] for c in cols], axis=0)
+        return jnp.dot(lhs, rhs, preferred_element_type=F32)
+
+    wait_kib(v3_rsem.at[0], 3072)
+    for r in range(AHEAD):
         arrive(r, 0)
         arrive(r, 1)
 
+        def begin(m, c, r=r):
+            early[r, chunk_rows(m), :] = some(r, m, (y, up, down))
+            return c
+
+        lax.fori_loop(0, NB * S // CHUNK, begin, 0)
+
+    for h in range(2):
+        wait_along(far, h)
+        to_core(far, h, 1)
+    wait_kib(v3_rsem.at[1], 1024)
+
+    for r in range(ROUNDS - 1):
+        if r >= AHEAD:
+            arrive(r, 0)
+            arrive(r, 1)
+
         def second_product(m, c, r=r):
-            done[chunk_rows(m), 2 * r : 2 * r + 2, :] = product(virt, recv, r, m)
+            rows = chunk_rows(m)
+            if r < AHEAD:
+                got = (early[r, rows, :] + some(r, m, (far,))).astype(BF16).reshape(CHUNK, 2, S)
+            else:
+                got = product(virt, recv, r, m)
+            done[rows, 2 * r : 2 * r + 2, :] = got
             return c
 
         lax.fori_loop(0, NB * S // CHUNK, second_product, 0)
@@ -418,6 +438,7 @@
             pltpu.VMEM((2, NB, S, 4 * S), BF16),
             pltpu.VMEM((ROUNDS, 2, 4, 2, S, 2 * S), BF16),
             pltpu.VMEM((256, 256), BF16),
+            pltpu.VMEM((AHEAD, NB * S, 2 * S), F32),
             dma((PL,)),
             dma((ROUNDS,)), dma((ROUNDS,)),
             dma(()), dma(()),
@@ -426,7 +447,7 @@
             dma(()), dma(()),
             dma(()), dma((2, 4)),
             dma((6,)), dma((4, 2)),
-            dma(()), dma(()),
+            dma(()), dma((2,)),
             dma((ROUNDS,)), dma((ROUNDS, 2)),
         ],
         compiler_params=pltpu.CompilerParams(

time: 90.9 us -> 89.7 us (0.987); the launches traced: 89.7 us -> 89.6 us
  no operation moved by 1% of the time
where the time goes in v5:
time: 89.7 us; the launch traced here: 89.6 us
  Pallas kernels  89.6 us (100%)
    pallas_call x1, Pallas kernels, shards(): pl.pallas_call(kernel, out_shape=[pltpu.VMEM((4, 4, S, NB * S), BF16), pl...  85.2 us
    pallas_call x1, Pallas kernels, shards(): pl.pallas_call(last_kernel, out_shape=jax.ShapeDtypeStruct((NB * S, PL, S...  4.44 us

profile of v5, /device:TPU:1, one launch (start us, length us, event | category | flops | bytes accessed | tf_op | source)
XLA Modules:
  0.0 89.6 jit_solution(6618428183985140200)
XLA Ops:
  0.0 85.2 %shard_map.64 = (bf16[4,4,128,2048]{3,2,1,0:T(8,128)(2,1)S(1)}, bf16[4,2048,256]{2,1,0:T(8,128)(2,1)S(1)}, bf16[2048,8,128]{2,1,0:T(8,128)(2,1)S(1)}) custom-call(bf16[128,8,16,128]{3,2,1,0:T(8,128)(2,1)} %bitcast.6, s32[1,16]{1,0:T(1,128)} %tmask_hbm.1, bf16[128,2,128]{2,1,0:T(2,128)(2,1)} %bitcast.7, s32[1,2]{1,0:T(1,128)} %omask_hbm.1, ...), custom_call_target="tpu_custom_call" | custom-call | flops 16106127360 | bytes 8388608 | tf_op jit(solution)/shard_map/pallas_call | solution.py:420
  85.2 4.4 %shard_map.65 = bf16[2048,8,128]{2,1,0:T(8,128)(2,1)} custom-call(bf16[4,4,128,2048]{3,2,1,0:T(8,128)(2,1)S(1)} %get-tuple-element.8.virt, bf16[4,2048,256]{2,1,0:T(8,128)(2,1)S(1)} %get-tuple-element.9.recv, bf16[2048,8,128]{2,1,0:T(8,128)(2,1)S(1)} %get-tuple-element.10.done), custom_call_target="tpu_custom_call" | custom-call | flops 2147483648 | bytes 4194304 | tf_op jit(solution)/shard_map/pallas_call | solution.py:461

commit v6 on v5

--- a/solution.py
+++ b/solution.py
@@ -279,6 +279,18 @@
             wait_block(i, at(i, ring(p + dp), ring(q + dq)))
         for yy in (far, up if i == 1 else down):
             wait_spread(i, yy)
+
+    def virt_along():
+        for i in range(2):
+            q = place[i][1]
+            for h in range(2):
+                wait_line(i, ring(q + 2), 2 + h, h)
+        along(y, 0, 3, 0)
+        along(y, 1, 1, 1)
+        along(y, 1, 3, 2)
+        along(y, 0, 1, 3)
+        to_core(y, 0)
+        to_core(y, 1)
 
     def first_product(r, c):
         theirs = tm.at[pl.ds(pl.multiple_of(r * 512 + (1 - k) * 256, 256), 256), :]
@@ -314,20 +326,11 @@
                             pltpu.make_async_copy(src, dst, rsem).start()
                     else:
                         away()
+            if j == 0 and isinstance(r, int):
+                virt_along()
         return c
 
     first_product(0, 0)
-    for i in range(2):
-        q = place[i][1]
-        for h in range(2):
-            wait_line(i, ring(q + 2), 2 + h, h)
-    along(y, 0, 3, 0)
-    along(y, 1, 1, 1)
-    along(y, 1, 3, 2)
-    along(y, 0, 1, 3)
-    to_core(y, 0)
-    to_core(y, 1)
-
     lax.fori_loop(1, ROUNDS, first_product, 0)
 
     wait_along(up, 0)

time: 89.7 us -> 89.8 us (level)
  no operation moved by 1% of the time
where the time goes in v6:
time: 89.8 us; the launch traced here: 89.7 us
  Pallas kernels  89.7 us (100%)
    pallas_call x1, Pallas kernels, shards(): pl.pallas_call(kernel, out_shape=[pltpu.VMEM((4, 4, S, NB * S), BF16), pl...  85.2 us
    pallas_call x1, Pallas kernels, shards(): pl.pallas_call(last_kernel, out_shape=jax.ShapeDtypeStruct((NB * S, PL, S...  4.44 us

profile of v6, /device:TPU:1, one launch (start us, length us, event | category | flops | bytes accessed | tf_op | source)
XLA Modules:
  0.0 89.7 jit_solution(13689528534126920413)
XLA Ops:
  0.0 85.2 %shard_map.64 = (bf16[4,4,128,2048]{3,2,1,0:T(8,128)(2,1)S(1)}, bf16[4,2048,256]{2,1,0:T(8,128)(2,1)S(1)}, bf16[2048,8,128]{2,1,0:T(8,128)(2,1)S(1)}) custom-call(bf16[128,8,16,128]{3,2,1,0:T(8,128)(2,1)} %bitcast.6, s32[1,16]{1,0:T(1,128)} %tmask_hbm.1, bf16[128,2,128]{2,1,0:T(2,128)(2,1)} %bitcast.7, s32[1,2]{1,0:T(1,128)} %omask_hbm.1, ...), custom_call_target="tpu_custom_call" | custom-call | flops 16106127360 | bytes 8388608 | tf_op jit(solution)/shard_map/pallas_call | solution.py:423
  85.2 4.4 %shard_map.65 = bf16[2048,8,128]{2,1,0:T(8,128)(2,1)} custom-call(bf16[4,4,128,2048]{3,2,1,0:T(8,128)(2,1)S(1)} %get-tuple-element.8.virt, bf16[4,2048,256]{2,1,0:T(8,128)(2,1)S(1)} %get-tuple-element.9.recv, bf16[2048,8,128]{2,1,0:T(8,128)(2,1)S(1)} %get-tuple-element.10.done), custom_call_target="tpu_custom_call" | custom-call | flops 2147483648 | bytes 4194304 | tf_op jit(solution)/shard_map/pallas_call | solution.py:464

commit v7 on v5

--- a/solution.py
+++ b/solution.py
@@ -271,8 +271,6 @@
         pass_line(i, ring(q + 1), 3, 2, 0)
         wait_line(i, ring(q + 3), 1)
         pass_line(i, ring(q + 3), 1, 3, 1)
-    relayout(2)
-    relayout(3)
     for i in range(2):
         p, q = place[i]
         for dq, dp in ((1, 3), (1, 2), (3, 0), (3, 1), (2, 0), (2, 1), (2, 2), (2, 3)):
@@ -328,6 +326,8 @@
     to_core(y, 0)
     to_core(y, 1)
 
+    relayout(2)
+    relayout(3)
     lax.fori_loop(1, ROUNDS, first_product, 0)
 
     wait_along(up, 0)

time: 89.7 us -> 90 us (level)
  no operation moved by 1% of the time
where the time goes in v7:
time: 90 us; the launch traced here: 89.9 us
  Pallas kernels  89.8 us (100%)
    pallas_call x1, Pallas kernels, shards(): pl.pallas_call(kernel, out_shape=[pltpu.VMEM((4, 4, S, NB * S), BF16), pl...  85.4 us
    pallas_call x1, Pallas kernels, shards(): pl.pallas_call(last_kernel, out_shape=jax.ShapeDtypeStruct((NB * S, PL, S...  4.44 us

profile of v7, /device:TPU:1, one launch (start us, length us, event | category | flops | bytes accessed | tf_op | source)
XLA Modules:
  0.0 89.9 jit_solution(3232936635788510907)
XLA Ops:
  0.0 85.4 %shard_map.64 = (bf16[4,4,128,2048]{3,2,1,0:T(8,128)(2,1)S(1)}, bf16[4,2048,256]{2,1,0:T(8,128)(2,1)S(1)}, bf16[2048,8,128]{2,1,0:T(8,128)(2,1)S(1)}) custom-call(bf16[128,8,16,128]{3,2,1,0:T(8,128)(2,1)} %bitcast.6, s32[1,16]{1,0:T(1,128)} %tmask_hbm.1, bf16[128,2,128]{2,1,0:T(2,128)(2,1)} %bitcast.7, s32[1,2]{1,0:T(1,128)} %omask_hbm.1, ...), custom_call_target="tpu_custom_call" | custom-call | flops 16106127360 | bytes 8388608 | tf_op jit(solution)/shard_map/pallas_call | solution.py:420
  85.4 4.4 %shard_map.65 = bf16[2048,8,128]{2,1,0:T(8,128)(2,1)} custom-call(bf16[4,4,128,2048]{3,2,1,0:T(8,128)(2,1)S(1)} %get-tuple-element.8.virt, bf16[4,2048,256]{2,1,0:T(8,128)(2,1)S(1)} %get-tuple-element.9.recv, bf16[2048,8,128]{2,1,0:T(8,128)(2,1)S(1)} %get-tuple-element.10.done), custom_call_target="tpu_custom_call" | custom-call | flops 2147483648 | bytes 4194304 | tf_op jit(solution)/shard_map/pallas_call | solution.py:461
